TPU v7x, 256 devices: a whole 4x4x8 slice. The times are simulated.
256 devices in a mesh: tok: 4 (over z_lo), ffn: 8 (over y, z_hi), wid: 8 (over x, core).
Axes of the slice: x: 4, y: 4, z: 8 (z_hi: 2, z_lo: 4; z = z_hi * 4 + z_lo), core: 2. Of those that a mesh axis runs over, the one named last changes fastest.
Arguments:
- grad_out: bfloat16 [4096, 8192], P(('tok', 'ffn'), 'wid'), may hold values from -6 to 6
- hidden: bfloat16 [4096, 14336], P(('tok', 'wid'), 'ffn'), may hold values from -0.09375 to 0.09375
- down_weight: bfloat16 [14336, 8192], P('ffn', 'wid'), may hold values from -0.046875 to 0.046875
Outputs:
- input_grad: bfloat16 [4096, 14336], P(('tok', 'wid'), 'ffn')
- weight_grad: float32 [4, 14336, 8, 256], P('tok', 'ffn', 'wid')
All inputs are finite; a program needn't handle non-finite values.
Results may differ from a plain program's by a relative error of at most 0.001.
Values may be sent and summed in bfloat16 or wider, within the bound.
A program may use at most 128 MiB of HBM per device.

v0:
```python
import jax
import jax.numpy as jnp
from jax import lax
from jax.sharding import PartitionSpec as P


def shards(grad_out, hidden, down_weight):
    grad_rows = lax.all_gather(grad_out, "ffn", axis=0, tiled=True)
    window = grad_rows
    input_grad = lax.psum_scatter(
        lax.dot_general(
            window, down_weight, (((1,), (1,)), ((), ())), preferred_element_type=jnp.float32
        ),
        "wid",
        scatter_dimension=0,
        tiled=True,
    ).astype(jnp.bfloat16)
    col_parts = lax.axis_size("tok")
    col_width = grad_rows.shape[1] // col_parts
    act_rows = lax.all_gather(hidden, "wid", axis=0, tiled=True)
    window = grad_rows
    window = window.reshape(window.shape[0], 1 * lax.axis_size("tok"), col_width)
    product = jnp.einsum("rf,rac->afc", act_rows, window, preferred_element_type=jnp.float32)
    weight_grad = lax.psum_scatter(product[:, :, None, :], "tok", scatter_dimension=0, tiled=True)
    return (input_grad, weight_grad)


def solution(mesh):
    placed = (P(("tok", "ffn"), "wid"), P(("tok", "wid"), "ffn"), P("ffn", "wid"))
    return jax.shard_map(
        shards,
        mesh=mesh,
        in_specs=placed,
        out_specs=(P(("tok", "wid"), "ffn"), P("tok", "ffn", "wid", None)),
        check_vma=False,
    )
```

profile of v0, /device:TPU:32, one launch (start us, length us, event | category | flops | bytes accessed | tf_op | source)
XLA Modules:
  0.0 318.4 jit_solution(15433782322718523018)
XLA Ops:
  7.2 0.0 all-gather.3.cloned.1.call-start
  7.2 0.7 all-gather.3.cloned.1.call-update
  7.9 0.0 all-gather.5.cloned.1.call-start
  7.9 0.7 all-gather.5.cloned.1.call-update
  8.6 0.0 reduce-scatter.3.cloned.1.call-start
  8.7 79.6 %all-gather.3.cloned.1.call-done = bf16[1024,1024]{1,0:T(8,128)(2,1)} async-done(((bf16[128,1024]{1,0:T(8,128)(2,1)}), bf16[1024,1024]{1,0:T(8,128)(2,1)}) %all-gather.3.cloned.1.call-update) | async-done | bytes 2097168 | tf_op jit(solution)/shard_map/all_gather | solution.py:8
  88.3 9.6 %fusion.1 = f32[1024,1792]{1,0:T(8,128)} fusion(bf16[1024,1024]{1,0:T(8,128)(2,1)} %all-gather.3.cloned.1.call-done, bf16[1792,1024]{1,0:T(8,128)(2,1)} %param.5), kind=kOutput, calls=%fused_computation.2 | convolution fusion | flops 3758096384 | bytes 13107200 | tf_op jit(solution)/shard_map/dot_general | solution.py:11
  97.9 0.0 copy-start
  97.9 0.0 reduce-scatter.3.cloned.1.call-update
  97.9 0.0 reduce-scatter.5.cloned.1.call-start
  98.0 1.6 copy-done
  99.6 2.5 copy.5
  102.1 17.2 %all-gather.5.cloned.1.call-done = bf16[1024,1792]{1,0:T(8,128)(2,1)} async-done(((bf16[128,1792]{1,0:T(8,128)(2,1)}), bf16[1024,1792]{1,0:T(8,128)(2,1)}) %all-gather.5.cloned.1.call-update) | async-done | bytes 3670032 | tf_op jit(solution)/shard_map/all_gather | solution.py:20
  119.4 9.6 %convolution_bitcast_fusion = f32[4,1792,1,256]{1,3,0,2:T(8,128)} fusion(bf16[1024,4,256]{0,2,1:T(8,128)(2,1)} %bitcast.11, bf16[1024,1792]{1,0:T(8,128)(2,1)} %all-gather.5.cloned.1.call-done), kind=kOutput, calls=%fused_computation | convolution fusion | flops 3758096384 | bytes 13107200 | tf_op jit(solution)/shard_map/rf,rac->afc/dot_general | solution.py:23
  129.0 0.0 reduce-scatter.5.cloned.1.call-update
  129.0 42.9 %reduce-scatter.3.cloned.1.call-done = f32[128,1792]{1,0:T(8,128)} async-done(((f32[1024,1792]{1,0:T(8,128)}), f32[128,1792]{1,0:T(8,128)}) %reduce-scatter.3.cloned.1.call-update) | async-done | bytes 917520 | tf_op jit(solution)/shard_map/reduce_scatter | solution.py:10
  171.9 2.0 convert_element_type.3
  173.9 133.0 %reduce-scatter.5.cloned.1.call-done = f32[1,1792,1,256]{1,3,0,2:T(8,128)} async-done(((f32[4,1792,1,256]{1,3,0,2:T(8,128)}), f32[1,1792,1,256]{1,3,0,2:T(8,128)}) %reduce-scatter.5.cloned.1.call-update) | async-done | bytes 1835024 | tf_op jit(solution)/shard_map/reduce_scatter | solution.py:24
  306.9 5.0 %copy.6 = f32[1,1792,1,256]{3,2,1,0:T(1,128)} copy(f32[1,1792,1,256]{1,3,0,2:T(8,128)} %reduce-scatter.5.cloned.1.call-done) | data formatting | bytes 3670016
Async XLA Ops:
  7.2 81.1 %all-gather.3.cloned.1.call-start = ((), (), s32[]{:S(2)}) async-start(), calls=%async_computation.2 | async-start | bytes 2359296 | tf_op jit(solution)/shard_map/all_gather | solution.py:8
  7.9 111.5 %all-gather.5.cloned.1.call-start = ((), (), s32[]{:S(2)}) async-start(), calls=%async_computation.4 | async-start | bytes 4128768 | tf_op jit(solution)/shard_map/all_gather | solution.py:20
  8.6 163.2 %reduce-scatter.3.cloned.1.call-start = ((), (), s32[]{:S(2)}) async-start(), calls=%async_computation.3 | async-start | bytes 8257536 | tf_op jit(solution)/shard_map/reduce_scatter | solution.py:10
  97.9 1.7 copy-start
  97.9 208.9 %reduce-scatter.5.cloned.1.call-start = ((), (), s32[]{:S(2)}) async-start(), calls=%async_computation.5 | async-start | bytes 9175040 | tf_op jit(solution)/shard_map/reduce_scatter | solution.py:24
Sparse Core Ops, SparseCore 0:
  10.6 77.6 all-gather.2
  90.1 29.2 all-gather.4
  121.9 49.9 reduce-scatter.2
  174.3 132.5 reduce-scatter.4
where the time goes:
time: 320 us; the launch traced here: 318 us
  waiting for transfers between devices  274 us (86%)
  matrix products  19.2 us (6%)
  between operations  13.8 us (4%)
  local copies, waits for them, and re-layouts  9.2 us (3%)
    reduce_scatter x1, waiting for transfers between devices, shards(): lax.psum_scatter(product[:, :, None, :], 'tok', scatter_dimension=0, tile...  133 us
    all_gather x1, waiting for transfers between devices, shards(): grad_rows = lax.all_gather(grad_out, 'ffn', axis=0, tiled=True)  79.6 us
    reduce_scatter x1, waiting for transfers between devices, shards(): lax.psum_scatter(lax.dot_general(window, down_weight, (((1,), (1,)), ((),...  42.9 us
    all_gather x1, waiting for transfers between devices, shards(): act_rows = lax.all_gather(hidden, 'wid', axis=0, tiled=True)  17.2 us
    dot_general x1, matrix products, shards(): jnp.einsum('rf,rac->afc', act_rows, window, preferred_element_type=jnp.fl...  9.63 us
    dot_general x1, matrix products, shards(): lax.dot_general(window, down_weight, (((1,), (1,)), ((), ())), preferred_...  9.61 us
    unnamed x3, local copies, waits for them, and re-layouts  6.67 us
  transfers between devices with their start and end apart: 4, of which 4 were waited for; matrix products, arithmetic and copies ran while one was open for 7% of the time, Pallas kernels for 0%

commit v1 on v0

v1 whole, which is shorter than its diff:
```python
import functools

import jax
import jax.numpy as jnp
from jax import lax
from jax.experimental import pallas as pl
from jax.experimental.pallas import tpu as pltpu
from jax.sharding import PartitionSpec as P

F32, BF16 = jnp.float32, jnp.bfloat16
MESH = pl.DeviceIdType.MESH
COLS = 256
ROWS = 128
PAD = 16
ORDER = (3, 2, 0, 1)


def encode(dst, value):
    top = jnp.max(jnp.abs(value), axis=0, keepdims=True)
    scale = (1.0 / jnp.maximum(top, 1e-30)).astype(BF16)
    wide = scale.astype(F32)
    step = 64
    for b in range(0, value.shape[0], step):
        u = value[b : b + step] * wide
        u2 = u * u
        dst[b : b + step, :] = (u * jnp.abs(u) * u2 * (u2 * u2)).astype(BF16)
    dst[value.shape[0] :, :] = jnp.broadcast_to(wide, (PAD, value.shape[1])).astype(BF16)


def decode(src, b, step):
    n = src.shape[0] - PAD
    back = 1.0 / src[n:, :].astype(F32)[0:1]
    y = src[b : b + step, :].astype(F32)
    r = lax.rsqrt(jnp.maximum(jnp.abs(y), 1.2e-38))
    r = lax.rsqrt(r)
    r = r * lax.rsqrt(r) * back
    return jnp.where(y == 0.0, 0.0, jnp.where(y < 0.0, -r, r))


def kernel(
    g_in, h_in, w_in, ig_out, wg_out,
    G, GS, H, HT, HU, W, WS, igp, igF, igB, igA, igo, wgs, wgr, wgo,
    gA, gBC, gZ4, gZ, gS, hA, hBC, hS, hZ, wS, iF, iB, iA, q, lW, lG, lH, lO, lP,
    sG, sGS, sH, sHS, sW, sI, sWG,
):
    n_m = H.shape[0]
    t, f, w = lax.axis_index("tok"), lax.axis_index("ffn"), lax.axis_index("wid")
    y, zh, x, c = f // 2, f % 2, w // 2, w % 2
    d = 1 - 2 * c
    half = t // 2
    mid = (t == 1) | (t == 2)
    end = jnp.logical_not(mid)
    xp, xs = lax.rem(x + d + 4, 4), lax.rem(x - d + 4, 4)
    yp, ys = lax.rem(y + d + 4, 4), lax.rem(y - d + 4, 4)
    x2 = lax.rem(x + 2, 4)
    to_xp, to_xs, to_sib = {"wid": xp * 2 + c}, {"wid": xs * 2 + c}, {"wid": x * 2 + 1 - c}
    to_yp, to_ys, to_z4 = {"ffn": yp * 2 + zh}, {"ffn": ys * 2 + zh}, {"ffn": y * 2 + 1 - zh}
    to_zp, to_zq = {"tok": t + 1 - 2 * (t % 2)}, {"tok": 3 - t}

    def send(src, dst, ssem, rsem, dev):
        pltpu.make_async_remote_copy(
            src_ref=src, dst_ref=dst, send_sem=ssem, recv_sem=rsem, device_id=dev, device_id_type=MESH
        ).start()

    def local(src, dst, sem):
        pltpu.make_async_copy(src, dst, sem).start()

    def wait(ref, sem):
        pltpu.make_async_copy(ref, ref, sem).wait()

    def cols(i):
        return pl.ds(pl.multiple_of(i * COLS, COLS), COLS)

    def rows(i, n=ROWS):
        return pl.ds(pl.multiple_of(i * n, n), n)

    def in_cols(j):
        base = jnp.where(j < 2, 3 - j, j - 2)
        return cols(base + half * (3 - 2 * base))

    def gblk(tr, z, yy, j):
        return G.at[rows(tr * 8 + z * 4 + yy), cols(j)]

    def hblk(m, tr, xx):
        return H.at[m, rows(tr * 8 + c * 4 + xx)]

    def zsel(s):
        return zh if s == 0 else 1 - zh

    barrier = pltpu.get_barrier_semaphore()
    for dev in (to_xp, to_xs, to_sib, to_yp, to_ys, to_z4, to_zp):
        pl.semaphore_signal(barrier, inc=1, device_id=dev, device_id_type=MESH)

    @pl.when(mid)
    def _():
        pl.semaphore_signal(barrier, inc=1, device_id=to_zq, device_id_type=MESH)
        pl.semaphore_wait(barrier, 8)

    @pl.when(end)
    def _():
        pl.semaphore_wait(barrier, 7)

    def own_y(j):
        send(g_in.at[:, in_cols(j)], gblk(0, zh, y, j), sG, gA.at[0, 0, j], to_yp)
        send(g_in.at[:, in_cols(j)], gblk(0, zh, y, j), sG, gBC.at[0, 0, j], to_ys)

    def own_x(m):
        send(h_in.at[:, cols(m)], hblk(m, 0, x), sH, hA.at[0, m], to_xp)
        send(h_in.at[:, cols(m)], hblk(m, 0, x), sH, hBC.at[0, m], to_xs)

    def own_z(m):
        send(h_in.at[:, cols(m)], hblk(m, 1, x), sH, hZ.at[m], to_zp)

    for j in range(4):
        send(g_in.at[:, in_cols(j)], gblk(0, zh, y, j), sG, gZ4.at[j], to_z4)
        if j != 2:

            @pl.when(end)
            def _():
                send(g_in.at[:, in_cols(j)], gblk(1, zh, y, j), sG, gZ.at[0, j], to_zp)

        if j == 0:
            own_x(0)

            @pl.when(end)
            def _():
                own_z(0)

    @pl.when(end)
    def _():
        own_z(1)

    for j in range(4):
        local(g_in.at[:, in_cols(j)], gblk(0, zh, y, j), lG)
    for m in range(n_m):
        local(h_in.at[:, cols(m)], hblk(m, 0, x), lH)
    for j in range(4):
        local(w_in.at[:, in_cols(j)], W.at[:, cols(j)], lW)
        send(w_in.at[:, in_cols(j)], WS.at[:, cols(j)], sW, wS, to_sib)
    wait(G.at[0:ROWS], lG)
    wait(H.at[:, 0:ROWS], lH)

    blk = G.at[0:ROWS, 0:COLS]
    two = G.at[0 : 2 * ROWS, 0:COLS]

    def spread_y(tr, s, j):
        z = zsel(s)
        send(gblk(tr, z, y, j), gblk(tr, z, y, j), sG, gA.at[tr, s, j], to_yp)
        send(gblk(tr, z, y, j), gblk(tr, z, y, j), sG, gBC.at[tr, s, j], to_ys)

    def pass_y(tr, s, j):
        z = zsel(s)
        wait(blk, gA.at[tr, s, j])
        send(gblk(tr, z, ys, j), gblk(tr, z, ys, j), sG, gBC.at[tr, s, j], to_yp)

    def step(s, _):
        @pl.when(s < n_m - 1)
        def _():
            own_x(s + 1)

        @pl.when(end & (s < n_m - 2))
        def _():
            own_z(s + 2)

        @pl.when(s < 4)
        def _():
            own_y(s)

            @pl.when(mid & (s != 2))
            def _():
                wait(blk, gZ.at[0, s])
                spread_y(1, 0, s)

        @pl.when(mid & (s < n_m))
        def _():
            wait(blk, hZ.at[s])
            send(hblk(s, 1, x), hblk(s, 1, x), sH, hA.at[1, s], to_xp)
            send(hblk(s, 1, x), hblk(s, 1, x), sH, hBC.at[1, s], to_xs)

        @pl.when(s < n_m)
        def _():
            wait(blk, hA.at[0, s])
            send(hblk(s, 0, xs), hblk(s, 0, xs), sH, hBC.at[0, s], to_xp)

        @pl.when(s < 4)
        def _():
            wait(blk, gZ4.at[s])
            spread_y(0, 1, s)

            @pl.when(end & (s != 2))
            def _():
                send(gblk(0, 1 - zh, y, s), gblk(1, 1 - zh, y, s), sG, gZ.at[1, s], to_zp)

            pass_y(0, 0, s)

        @pl.when((s >= 1) & (s < 5))
        def _():
            j = s - 1

            @pl.when(mid & (j != 2))
            def _():
                wait(blk, gZ.at[1, j])
                spread_y(1, 1, j)
                pass_y(1, 0, j)

            pass_y(0, 1, j)

        @pl.when((s >= 1) & (s < n_m + 1))
        def _():
            m = s - 1

            @pl.when(mid)
            def _():
                wait(blk, hA.at[1, m])
                send(hblk(m, 1, xs), hblk(m, 1, xs), sH, hBC.at[1, m], to_xp)

            wait(two, hBC.at[0, m])
            own = H.at[m, rows(c, 4 * ROWS)]
            send(own, own, sHS, hS.at[0, m], to_sib)

        @pl.when((s >= 2) & (s < n_m + 2) & mid)
        def _():
            m = s - 2
            wait(two, hBC.at[1, m])
            own = H.at[m, rows(2 + c, 4 * ROWS)]
            send(own, own, sHS, hS.at[1, m], to_sib)

        @pl.when((s >= 2) & (s < 6))
        def _():
            j = s - 2

            @pl.when(mid & (j != 2))
            def _():
                pass_y(1, 1, j)

        @pl.when((s >= 3) & (s < 7))
        def _():
            j = s - 3
            wait(two, gBC.at[0, 0, j])
            wait(two, gBC.at[0, 1, j])

            @pl.when(mid & (j != 2))
            def _():
                wait(two, gBC.at[1, 0, j])
                wait(two, gBC.at[1, 1, j])

            send(G.at[rows(1 - c, 4 * ROWS), cols(j)], GS.at[:, cols(j)], sGS, gS, to_sib)

        @pl.when((s >= 3) & (s < n_m + 3))
        def _():
            m = s - 3
            wait(H.at[0, 0 : 4 * ROWS], hS.at[0, m])

            @pl.when(mid)
            def _():
                wait(H.at[0, 0 : 4 * ROWS], hS.at[1, m])
                HT[m % 2] = H[m].T
                encode(wgs.at[0, m], jnp.dot(HT[m % 2], G[:, 0:COLS], preferred_element_type=F32))
                send(wgs.at[0, m], wgr.at[0, m], sWG, q.at[0, m], to_zq)

        @pl.when(mid & (s >= 4) & (s < n_m + 4))
        def _():
            m = s - 4
            encode(wgs.at[1, m], jnp.dot(HT[m % 2], G[:, COLS : 2 * COLS], preferred_element_type=F32))
            send(wgs.at[1, m], wgr.at[1, m], sWG, q.at[1, m], to_zq)

        @pl.when(s == n_m)
        def _():
            wait(W, lW)
            wait(WS, wS)
            wait(GS, gS)

        @pl.when((s >= n_m) & (s < 2 * n_m))
        def _():
            i = s - n_m
            nt = (((1,), (1,)), ((), ()))
            part = lax.dot_general(G[rows(c, 4 * ROWS), :], W[cols(i), :], nt, preferred_element_type=F32)
            part += lax.dot_general(GS[...], WS[cols(i), :], nt, preferred_element_type=F32)
            igp[i] = part.reshape(4, ROWS, COLS)
            send(igp.at[i, x2], igF.at[i], sI, iF.at[i], to_xp)
            send(igp.at[i, xs], igB.at[i], sI, iB.at[i], to_xs)

        @pl.when((s >= n_m + 1) & (s < 2 * n_m + 1))
        def _():
            i = s - n_m - 1
            wait(igF.at[i], iF.at[i])
            igp[i, xp] = igp[i, xp] + igF[i]
            send(igp.at[i, xp], igA.at[i], sI, iA.at[i], to_xp)

        @pl.when(s >= n_m + 2)
        def _():
            i = s - n_m - 2
            wait(igB.at[i], iB.at[i])
            wait(igA.at[i], iA.at[i])
            igo[i] = (igp[i, x] + igB[i] + igA[i]).astype(BF16)
            local(igo.at[i], ig_out.at[:, cols(i)], lO)

        @pl.when(mid & (s >= n_m) & (s < 2 * n_m))
        def _():
            u = s - n_m
            HU[...] = H[u].T
            part = jnp.dot(HU[:, 0 : 8 * ROWS], G[0 : 8 * ROWS, 2 * COLS : 3 * COLS], preferred_element_type=F32)
            wait(wgr.at[0, u], q.at[0, u])
            encode(wgs.at[2, u], part + decode(wgr.at[0, u], 0, COLS))
            send(wgs.at[2, u], wgr.at[2, u], sWG, q.at[2, u], to_zp)
            part = jnp.dot(HU[...], G[:, 3 * COLS :], preferred_element_type=F32)
            wait(wgr.at[1, u], q.at[1, u])
            wgo[u] = part + decode(wgr.at[1, u], 0, COLS)
            local(wgo.at[u], wg_out.at[cols(u)], lP)

        @pl.when(end & (s >= n_m + 1) & (s < 2 * n_m + 1))
        def _():
            u = s - n_m - 1
            HU[:, 0 : 8 * ROWS] = H[u, 0 : 8 * ROWS].T
            part = jnp.dot(HU[:, 0 : 8 * ROWS], G[0 : 8 * ROWS, 2 * COLS : 3 * COLS], preferred_element_type=F32)
            wait(wgr.at[2, u], q.at[2, u])
            wgo[u] = part + decode(wgr.at[2, u], 0, COLS)
            local(wgo.at[u], wg_out.at[cols(u)], lP)

        return 0

    lax.fori_loop(0, 2 * n_m + 2, step, 0)

    @pl.when(mid)
    def _():
        wait(G.at[0 : 46 * ROWS // 4], sG)
        wait(H.at[:, 0 : 6 * ROWS], sH)
        wait(H.at[:, 0 : 8 * ROWS], sHS)
        wait(wgs, sWG)

    @pl.when(end)
    def _():
        wait(G.at[0 : 34 * ROWS // 4], sG)
        wait(H.at[:, 0 : 4 * ROWS], sH)
        wait(H.at[:, 0 : 4 * ROWS], sHS)

    wait(GS, sGS)
    wait(W, sW)
    wait(igp.at[:, 0:3], sI)
    wait(igo, lO)
    wait(wgo, lP)


def shards(grad_out, hidden, down_weight):
    n_m = hidden.shape[1] // COLS
    dma = pltpu.SemaphoreType.DMA
    vm = pltpu.VMEM
    coded = (3, n_m, COLS + PAD, COLS)
    ig, wg = pl.pallas_call(
        kernel,
        out_shape=(
            jax.ShapeDtypeStruct((ROWS, n_m * COLS), BF16),
            jax.ShapeDtypeStruct((n_m * COLS, COLS), F32),
        ),
        in_specs=[pl.BlockSpec(memory_space=pl.ANY)] * 3,
        out_specs=(pl.BlockSpec(memory_space=pl.ANY),) * 2,
        scratch_shapes=[
            vm((16 * ROWS, 4 * COLS), BF16),
            vm((4 * ROWS, 4 * COLS), BF16),
            vm((n_m, 16 * ROWS, COLS), BF16),
            vm((2, COLS, 16 * ROWS), BF16),
            vm((COLS, 16 * ROWS), BF16),
            vm((n_m * COLS, 4 * COLS), BF16),
            vm((n_m * COLS, 4 * COLS), BF16),
            vm((n_m, 4, ROWS, COLS), F32),
            vm((n_m, ROWS, COLS), F32),
            vm((n_m, ROWS, COLS), F32),
            vm((n_m, ROWS, COLS), F32),
            vm((n_m, ROWS, COLS), BF16),
            vm(coded, BF16),
            vm(coded, BF16),
            vm((n_m, COLS, COLS), F32),
            dma((2, 2, 4)), dma((2, 2, 4)), dma((4,)), dma((2, 4)), dma,
            dma((2, n_m)), dma((2, n_m)), dma((2, n_m)), dma((n_m,)), dma,
            dma((n_m,)), dma((n_m,)), dma((n_m,)), dma((3, n_m)),
            dma, dma, dma, dma, dma,
            dma, dma, dma, dma, dma, dma, dma,
        ],
        compiler_params=pltpu.CompilerParams(
            collective_id=0, has_side_effects=True, vmem_limit_bytes=60 * 2**20
        ),
        cost_estimate=pl.CostEstimate(flops=12 * 10**9, bytes_accessed=10**7, transcendentals=0),
    )(grad_out, hidden, down_weight)
    return ig, wg[None, :, None, :]


def solution(mesh):
    placed = (P(("tok", "ffn"), "wid"), P(("tok", "wid"), "ffn"), P("ffn", "wid"))
    return jax.shard_map(
        shards,
        mesh=mesh,
        in_specs=placed,
        out_specs=(P(("tok", "wid"), "ffn"), P("tok", "ffn", "wid", None)),
        check_vma=False,
    )
```

time: 320 us -> 111 us (0.35)
  waiting for transfers between devices: 274 us -> 0 us
  Pallas kernels: 0 us -> 103 us
  matrix products: 19.2 us -> 0 us
  between operations: 13.8 us -> 0.65 us
    reduce_scatter x2 -> x0, waiting for transfers between devices: 176 us -> none  [the longest x1 133 us: shards(): lax.psum_scatter(product[:, :, None, :], 'tok', scatter_dimension=0, tile...]
    pallas_call x0 -> x1, Pallas kernels: none -> 103 us  [shards(): pl.pallas_call(kernel, out_shape=(jax.ShapeDtypeStruct((ROWS, n_m * COLS)...]
    all_gather x2 -> x0, waiting for transfers between devices: 96.8 us -> none  [the longest x1 79.6 us: shards(): grad_rows = lax.all_gather(grad_out, 'ffn', axis=0, tiled=True)]
    dot_general x2 -> x0, matrix products: 19.2 us -> none  [the longest x1 9.63 us: shards(): jnp.einsum('rf,rac->afc', act_rows, window, preferred_element_type=jnp.fl...]
    unnamed x3 -> x4, local copies, waits for them, and re-layouts: 6.67 us -> 6.97 us
  transfers between devices with their start and end apart: 4 -> 0, of which waited for: 4 -> 0; matrix products, arithmetic and copies ran while one was open for 7% -> 0% of each run, Pallas kernels for 0% -> 0%
where the time goes in v1:
time: 111 us
  Pallas kernels  103 us (93%)
  local copies, waits for them, and re-layouts  6.97 us (6%)
    pallas_call x1, Pallas kernels, shards(): pl.pallas_call(kernel, out_shape=(jax.ShapeDtypeStruct((ROWS, n_m * COLS)...  103 us
    unnamed x4, local copies, waits for them, and re-layouts  6.97 us

profile of v1, /device:TPU:32, one launch (start us, length us, event | category | flops | bytes accessed | tf_op | source)
XLA Modules:
  0.0 110.6 jit_solution(3139440022469193205)
XLA Ops:
  0.6 103.0 %shard_map.50 = (bf16[128,1792]{1,0:T(8,128)(2,1)}, f32[1792,256]{1,0:T(8,128)}) custom-call(bf16[128,1024]{1,0:T(8,128)(2,1)} %g_in.1, bf16[128,1792]{1,0:T(8,128)(2,1)} %h_in.1, bf16[1792,1024]{1,0:T(8,128)(2,1)} %w_in.1), custom_call_target="tpu_custom_call" | custom-call | flops 12000000000 | bytes 10000000 | tf_op jit(solution)/shard_map/pallas_call | solution.py:349
  103.6 0.0 copy-start
  103.6 6.2 %copy.5 = f32[1,1792,1,256]{3,2,1,0:T(1,128)} copy(f32[1,1792,1,256]{3,1,2,0:T(8,128)} %bitcast.1) | data formatting | bytes 3670016
  109.8 0.0 copy-done
  109.8 0.8 copy.7
Async XLA Ops:
  103.6 6.2 %copy-start = (bf16[128,1792]{1,0:T(8,128)(2,1)S(1)}, bf16[128,1792]{1,0:T(8,128)(2,1)}, u32[]{:S(2)}) copy-start(bf16[128,1792]{1,0:T(8,128)(2,1)} %get-tuple-element.10) | copy-start | bytes 1376260

commit v2 on v0

v2 whole, which is shorter than its diff:
```python
import functools

import jax
import jax.numpy as jnp
from jax import lax
from jax.experimental import pallas as pl
from jax.experimental.pallas import tpu as pltpu
from jax.sharding import PartitionSpec as P

F32, BF16 = jnp.float32, jnp.bfloat16
MESH = pl.DeviceIdType.MESH
COLS = 256
ROWS = 128
PAD = 16
SPAN = 240.0
ARRIVE = (-3, 0, 2, 3)
STRAIGHT = (0, 1)
LAG = 3
FIRST = 6


def encode(dst, value):
    n = value.shape[0]
    top = jnp.max(jnp.abs(value), axis=0, keepdims=True)
    scale = (1.0 / jnp.maximum(top, 1e-30)).astype(BF16).astype(F32)
    for b in range(0, n, 64):
        u = value[b : b + 64] * scale
        y = jnp.exp2(jnp.abs(u) * SPAN - SPAN / 2)
        dst[b : b + 64, :] = jnp.where(u < 0.0, -y, y).astype(BF16)
    dst[n:, :] = jnp.broadcast_to(scale, (PAD, value.shape[1])).astype(BF16)


def decode(src):
    n = src.shape[0] - PAD
    scale = src[n:, :].astype(F32)[0:1]
    y = src[0:n, :].astype(F32)
    u = (jnp.log2(jnp.abs(y)) + SPAN / 2) * (1.0 / (SPAN * scale))
    return jnp.where(y < 0.0, -u, u)


def kernel(
    g_in, h_in, w_in, ig_out, wg_out,
    G, GS, H, HT, W, WS, igp, igs, igr, igo, wgs, wgr, wgo,
    gA, gBC, gZ4, gZ, gS, hA, hBC, hS, hZ, wS, iR, q, lW, lG, lH, lO, lP,
    sG, sGS, sH, sHS, sW, sI, sWG,
):
    n_m = H.shape[0]
    t, f, w = lax.axis_index("tok"), lax.axis_index("ffn"), lax.axis_index("wid")
    y, zh, x, c = f // 2, f % 2, w // 2, w % 2
    d = 1 - 2 * c
    half = t // 2
    mid = (t == 1) | (t == 2)
    end = jnp.logical_not(mid)
    xp, xs = lax.rem(x + d + 4, 4), lax.rem(x - d + 4, 4)
    yp, ys = lax.rem(y + d + 4, 4), lax.rem(y - d + 4, 4)
    x2, y2 = lax.rem(x + 2, 4), lax.rem(y + 2, 4)
    to_xp, to_xs, to_sib = {"wid": xp * 2 + c}, {"wid": xs * 2 + c}, {"wid": x * 2 + 1 - c}
    to_x2, to_y2 = {"wid": x2 * 2 + c}, {"ffn": y2 * 2 + zh}
    to_yp, to_ys, to_z4 = {"ffn": yp * 2 + zh}, {"ffn": ys * 2 + zh}, {"ffn": y * 2 + 1 - zh}
    near = t + 1 - 2 * (t % 2)
    to_zp, to_zq, to_zd = {"tok": near}, {"tok": 3 - t}, {"tok": near, "ffn": y * 2 + 1 - zh}

    def send(src, dst, ssem, rsem, dev):
        pltpu.make_async_remote_copy(
            src_ref=src, dst_ref=dst, send_sem=ssem, recv_sem=rsem, device_id=dev, device_id_type=MESH
        ).start()

    def local(src, dst, sem):
        pltpu.make_async_copy(src, dst, sem).start()

    def wait(ref, sem):
        pltpu.make_async_copy(ref, ref, sem).wait()

    def cols(i):
        return pl.ds(pl.multiple_of(i * COLS, COLS), COLS)

    def rows(i, n=ROWS):
        return pl.ds(pl.multiple_of(i * n, n), n)

    def in_cols(j):
        base = jnp.where(j < 2, 3 - j, j - 2)
        return cols(base + half * (3 - 2 * base))

    def gblk(tr, z, yy, j):
        return G.at[rows(tr * 8 + z * 4 + yy), cols(j)]

    def hblk(m, tr, xx):
        return H.at[m, rows(tr * 8 + c * 4 + xx)]

    def zsel(s):
        return zh if s == 0 else 1 - zh

    def to_ring_y(src, tr, s, j):
        dst = gblk(tr, zsel(s), y, j)
        if j in STRAIGHT:
            for dev in (to_yp, to_ys, to_y2):
                send(src, dst, sG, gBC.at[tr, s, j], dev)
        else:
            send(src, dst, sG, gA.at[tr, s, j], to_yp)
            send(src, dst, sG, gBC.at[tr, s, j], to_ys)

    def own_y(j):
        to_ring_y(g_in.at[:, in_cols(j)], 0, 0, j)

    def to_ring_x(src, tr, m):
        dst = hblk(m, tr, x)
        if isinstance(m, int) and m == 0:
            for dev in (to_xp, to_xs, to_x2):
                send(src, dst, sH, hBC.at[tr, m], dev)
        else:
            send(src, dst, sH, hA.at[tr, m], to_xp)
            send(src, dst, sH, hBC.at[tr, m], to_xs)

    def own_x(m):
        to_ring_x(h_in.at[:, cols(m)], 0, m)

    def own_z(m):
        send(h_in.at[:, cols(m)], hblk(m, 1, x), sH, hZ.at[m], to_zp)

    def own_z4(j):
        send(g_in.at[:, in_cols(j)], gblk(0, zh, y, j), sG, gZ4.at[j], to_z4)

    def own_gz(j):
        send(g_in.at[:, in_cols(j)], gblk(1, zh, y, j), sG, gZ.at[0, j], to_zp)

    for j in range(4):
        local(g_in.at[:, in_cols(j)], gblk(0, zh, y, j), lG)
        local(w_in.at[:, in_cols(j)], W.at[:, cols(j)], lW)
    for m in range(n_m):
        local(h_in.at[:, cols(m)], hblk(m, 0, x), lH)

    barrier = pltpu.get_barrier_semaphore()
    for dev in (to_xp, to_xs, to_x2, to_sib, to_yp, to_ys, to_y2, to_z4, to_zp, to_zd):
        pl.semaphore_signal(barrier, inc=1, device_id=dev, device_id_type=MESH)

    @pl.when(mid)
    def _():
        pl.semaphore_signal(barrier, inc=1, device_id=to_zq, device_id_type=MESH)
        pl.semaphore_wait(barrier, 11)

    @pl.when(end)
    def _():
        pl.semaphore_wait(barrier, 10)

    own_z4(0)
    own_x(0)
    own_y(0)
    own_x(1)
    own_x(2)

    @pl.when(end)
    def _():
        own_gz(0)
        own_z(0)
        send(g_in.at[:, in_cols(0)], gblk(1, zh, y, 0), sG, gZ.at[1, 0], to_zd)

    wait(G.at[0:ROWS], lG)
    wait(H.at[:, 0:ROWS], lH)

    blk = G.at[0:ROWS, 0:COLS]
    two = G.at[0 : 2 * ROWS, 0:COLS]
    three = G.at[0 : 3 * ROWS, 0:COLS]

    def spread_y(tr, s, j):
        to_ring_y(gblk(tr, zsel(s), y, j), tr, s, j)

    def full_y(tr, j):
        for s in range(2):
            wait(three if j in STRAIGHT else two, gBC.at[tr, s, j])

    def pass_y(tr, s, j):
        z = zsel(s)
        wait(blk, gA.at[tr, s, j])
        send(gblk(tr, z, ys, j), gblk(tr, z, ys, j), sG, gBC.at[tr, s, j], to_yp)

    def near_x(m):
        wait(blk, hA.at[0, m])
        send(hblk(m, 0, xs), hblk(m, 0, xs), sH, hBC.at[0, m], to_xp)

    def spread_x(m):
        wait(blk, hZ.at[m])
        to_ring_x(hblk(m, 1, x), 1, m)

    def pass_x(m):
        wait(blk, hA.at[1, m])
        send(hblk(m, 1, xs), hblk(m, 1, xs), sH, hBC.at[1, m], to_xp)

    def share(tr, m):
        wait(three if isinstance(m, int) and m == 0 else two, hBC.at[tr, m])
        own = H.at[m, rows(2 * tr + c, 4 * ROWS)]
        send(own, own, sHS, hS.at[tr, m], to_sib)

    def share_g(j):
        full_y(0, j)
        send(G.at[rows(1 - c, 4 * ROWS), cols(j)], GS.at[:, cols(j)], sGS, gS, to_sib)

    wait(blk, gZ4.at[0])
    spread_y(0, 1, 0)
    own_z4(1)

    @pl.when(end)
    def _():
        own_z(1)
        own_gz(1)

    @pl.when(mid)
    def _():
        wait(blk, gZ.at[0, 0])
        spread_y(1, 0, 0)
        wait(blk, gZ.at[1, 0])
        spread_y(1, 1, 0)
        spread_x(0)

    own_z4(2)
    own_y(1)
    near_x(1)
    own_x(3)
    share(0, 0)
    near_x(2)

    @pl.when(end)
    def _():
        own_z(2)

    @pl.when(mid)
    def _():
        spread_x(1)
        share(1, 0)

    share_g(0)

    def step(s, _):
        def at(k):
            return pl.when(s == k)

        @pl.when(s < n_m - 4)
        def _():
            own_x(s + 4)

        @pl.when(s < n_m - 3)
        def _():
            near_x(s + 3)

        @pl.when(end & (s < n_m - 3))
        def _():
            own_z(s + 3)

        @pl.when(mid & (s < n_m - 2))
        def _():
            spread_x(s + 2)

        @pl.when(s < n_m - 1)
        def _():
            @pl.when(mid)
            def _():
                pass_x(s + 1)

            share(0, s + 1)

        @pl.when(mid & (s >= 1) & (s < n_m))
        def _():
            share(1, s)

        @pl.when(mid & (s == 0))
        def _():
            full_y(1, 0)

        @pl.when(s < n_m)
        def _():
            wait(H.at[0, 0 : 4 * ROWS], hS.at[0, s])

            @pl.when(mid)
            def _():
                wait(H.at[0, 0 : 4 * ROWS], hS.at[1, s])
                HT[s] = H[s].T
                encode(wgs.at[0, s], jnp.dot(HT[s], G[:, 0:COLS], preferred_element_type=F32))
                send(wgs.at[0, s], wgr.at[0, s], sWG, q.at[0, s], to_zq)

        for j, k in ((1, LAG), (3, ARRIVE[3] + 3)):

            @pl.when(mid & (s == k))
            def _():
                full_y(1, j)

        @pl.when(mid & (s >= LAG) & (s < n_m + LAG))
        def _():
            m = s - LAG
            encode(wgs.at[1, m], jnp.dot(HT[m], G[:, COLS : 2 * COLS], preferred_element_type=F32))
            send(wgs.at[1, m], wgr.at[1, m], sWG, q.at[1, m], to_zq)

        for j in (1, 2, 3):
            both = j != 2
            relay = j not in STRAIGHT

            @at(ARRIVE[j] + 2)
            def _():
                if both and relay:

                    @pl.when(mid)
                    def _():
                        pass_y(1, 1, j)

                share_g(j)

            @at(ARRIVE[j] + 1)
            def _():
                if both:

                    @pl.when(mid)
                    def _():
                        wait(blk, gZ.at[1, j])
                        spread_y(1, 1, j)
                        if relay:
                            pass_y(1, 0, j)

                if relay:
                    pass_y(0, 1, j)

            @at(ARRIVE[j])
            def _():
                wait(blk, gZ4.at[j])
                spread_y(0, 1, j)

                if both:

                    @pl.when(end)
                    def _():
                        send(gblk(0, 1 - zh, y, j), gblk(1, 1 - zh, y, j), sG, gZ.at[1, j], to_zp)

                    @pl.when(mid)
                    def _():
                        wait(blk, gZ.at[0, j])
                        spread_y(1, 0, j)

                if relay:
                    pass_y(0, 0, j)

                if j == 1:
                    own_z4(3)
                    own_y(2)

                    @pl.when(end)
                    def _():
                        own_gz(3)

                if j == 2:
                    own_y(3)

        @at(0)
        def _():
            wait(W, lW)

        @pl.when(s < 4)
        def _():
            send(W.at[:, cols(s)], WS.at[:, cols(s)], sW, wS, to_sib)

        @at(FIRST)
        def _():
            wait(WS, wS)
            wait(GS, gS)

        for k in range(2):
            i = 2 * (s - FIRST) + k

            @pl.when((i >= 0) & (i < n_m))
            def _():
                nt = (((1,), (1,)), ((), ()))
                part = lax.dot_general(G[rows(c, 4 * ROWS), :], W[cols(i), :], nt, preferred_element_type=F32)
                part += lax.dot_general(GS[...], WS[cols(i), :], nt, preferred_element_type=F32)
                igp[i] = part.reshape(4, ROWS, COLS)
                encode(igs.at[0, i], igp[i, x2])
                send(igs.at[0, i], igr.at[0, i], sI, iR.at[0, i], to_xp)
                encode(igs.at[1, i], igp[i, xs])
                send(igs.at[1, i], igr.at[1, i], sI, iR.at[1, i], to_xs)

        for k in range(2):
            l = 2 * (s - FIRST - 1) + k

            @pl.when((l >= 0) & (l < n_m))
            def _():
                wait(igr.at[0, l], iR.at[0, l])
                encode(igs.at[2, l], igp[l, xp] + decode(igr.at[0, l]))
                send(igs.at[2, l], igr.at[2, l], sI, iR.at[2, l], to_xp)

        for k in range(2):
            n = 2 * (s - FIRST - 2) + k

            @pl.when((n >= 0) & (n < n_m))
            def _():
                wait(igr.at[1, n], iR.at[1, n])
                wait(igr.at[2, n], iR.at[2, n])
                igo[n] = (igp[n, x] + decode(igr.at[1, n]) + decode(igr.at[2, n])).astype(BF16)
                local(igo.at[n], ig_out.at[:, cols(n)], lO)

        def store(u, value):
            for l in range(2):
                wgo[u, pl.ds(l, COLS, stride=2), :] = value[:, l * ROWS : (l + 1) * ROWS]
            local(wgo.at[u], wg_out.at[rows(u, 2 * COLS)], lP)

        @pl.when(mid & (s >= 4) & (s < n_m + 4))
        def _():
            u = s - 4
            part = jnp.dot(HT[u, :, 0 : 8 * ROWS], G[0 : 8 * ROWS, 2 * COLS : 3 * COLS], preferred_element_type=F32)
            wait(wgr.at[0, u], q.at[0, u])
            encode(wgs.at[2, u], part + decode(wgr.at[0, u]))
            send(wgs.at[2, u], wgr.at[2, u], sWG, q.at[2, u], to_zp)

        @pl.when(mid & (s >= 6) & (s < n_m + 6))
        def _():
            u = s - 6
            part = jnp.dot(HT[u], G[:, 3 * COLS :], preferred_element_type=F32)
            wait(wgr.at[1, u], q.at[1, u])
            store(u, part + decode(wgr.at[1, u]))

        @pl.when(end & (s >= 6) & (s < n_m + 6))
        def _():
            u = s - 6
            part = jnp.dot(H[u, 0 : 8 * ROWS].T, G[0 : 8 * ROWS, 2 * COLS : 3 * COLS], preferred_element_type=F32)
            wait(wgr.at[2, u], q.at[2, u])
            store(u, part + decode(wgr.at[2, u]))

        return 0

    lax.fori_loop(0, n_m + 6, step, 0)

    @pl.when(mid)
    def _():
        wait(G.at[0 : 46 * ROWS // 4], sG)
        wait(H.at[:, 0 : 6 * ROWS], sH)
        wait(H.at[:, 0 : 8 * ROWS], sHS)
        wait(wgs, sWG)

    @pl.when(end)
    def _():
        wait(G.at[0 : 34 * ROWS // 4], sG)
        wait(H.at[:, 0 : 4 * ROWS], sH)
        wait(H.at[:, 0 : 4 * ROWS], sHS)

    wait(GS, sGS)
    wait(W, sW)
    wait(igs, sI)
    wait(igo, lO)
    wait(wgo, lP)


def place(ig, wg, ig_out, wg_out, sems):
    copies = [pltpu.make_async_copy(ig, ig_out, sems.at[0]), pltpu.make_async_copy(wg, wg_out, sems.at[1])]
    for copy in copies:
        copy.start()
    for copy in copies:
        copy.wait()


def shards(grad_out, hidden, down_weight):
    n_m = hidden.shape[1] // COLS
    dma = pltpu.SemaphoreType.DMA
    vm = pltpu.VMEM
    coded = (3, n_m, COLS + PAD, COLS)
    ig, wg = pl.pallas_call(
        kernel,
        out_shape=(
            jax.ShapeDtypeStruct((ROWS, n_m * COLS), BF16),
            jax.ShapeDtypeStruct((n_m * COLS * 2, ROWS), F32),
        ),
        in_specs=[pl.BlockSpec(memory_space=pl.ANY)] * 3,
        out_specs=(pl.BlockSpec(memory_space=pl.ANY),) * 2,
        scratch_shapes=[
            vm((16 * ROWS, 4 * COLS), BF16),
            vm((4 * ROWS, 4 * COLS), BF16),
            vm((n_m, 16 * ROWS, COLS), BF16),
            vm((n_m, COLS, 16 * ROWS), BF16),
            vm((n_m * COLS, 4 * COLS), BF16),
            vm((n_m * COLS, 4 * COLS), BF16),
            vm((n_m, 4, ROWS, COLS), F32),
            vm((3, n_m, ROWS + PAD, COLS), BF16),
            vm((3, n_m, ROWS + PAD, COLS), BF16),
            vm((n_m, ROWS, COLS), BF16),
            vm(coded, BF16),
            vm(coded, BF16),
            vm((n_m, 2 * COLS, ROWS), F32),
            dma((2, 2, 4)), dma((2, 2, 4)), dma((4,)), dma((2, 4)), dma,
            dma((2, n_m)), dma((2, n_m)), dma((2, n_m)), dma((n_m,)), dma,
            dma((3, n_m)), dma((3, n_m)),
            dma, dma, dma, dma, dma,
            dma, dma, dma, dma, dma, dma, dma,
        ],
        compiler_params=pltpu.CompilerParams(
            collective_id=0, has_side_effects=True, vmem_limit_bytes=60 * 2**20
        ),
        cost_estimate=pl.CostEstimate(flops=12 * 10**9, bytes_accessed=10**7, transcendentals=0),
    )(grad_out, hidden, down_weight)
    ig, wg = pl.pallas_call(
        place,
        out_shape=tuple(jax.ShapeDtypeStruct(a.shape, a.dtype) for a in (ig, wg)),
        in_specs=[pl.BlockSpec(memory_space=pltpu.VMEM)] * 2,
        out_specs=(pl.BlockSpec(memory_space=pl.ANY),) * 2,
        scratch_shapes=[dma((2,))],
    )(ig, wg)
    return ig, wg.reshape(1, n_m * COLS, 1, COLS)


def solution(mesh):
    placed = (P(("tok", "ffn"), "wid"), P(("tok", "wid"), "ffn"), P("ffn", "wid"))
    return jax.shard_map(
        shards,
        mesh=mesh,
        in_specs=placed,
        out_specs=(P(("tok", "wid"), "ffn"), P("tok", "ffn", "wid", None)),
        check_vma=False,
    )
```

time: 320 us -> 88.8 us (0.28)
  the two profiles are of different devices: /device:TPU:32 before, /device:TPU:2 now
where the time goes in v2:
time: 88.8 us; the launch traced here: 88.7 us
  Pallas kernels  88 us (99%)
    pallas_call x1, Pallas kernels, shards(): pl.pallas_call(kernel, out_shape=(jax.ShapeDtypeStruct((ROWS, n_m * COLS)...  85 us
    pallas_call x1, Pallas kernels, shards(): pl.pallas_call(place, out_shape=tuple((jax.ShapeDtypeStruct(a.shape, a.dt...  3.05 us

profile of v2, /device:TPU:2, one launch (start us, length us, event | category | flops | bytes accessed | tf_op | source)
XLA Modules:
  0.0 88.7 jit_solution(7742004999850785845)
XLA Ops:
  0.6 85.0 %shard_map.50 = (bf16[128,1792]{1,0:T(8,128)(2,1)}, f32[3584,128]{1,0:T(8,128)}) custom-call(bf16[128,1024]{1,0:T(8,128)(2,1)} %g_in.1, bf16[128,1792]{1,0:T(8,128)(2,1)} %h_in.1, bf16[1792,1024]{1,0:T(8,128)(2,1)} %w_in.1), custom_call_target="tpu_custom_call" | custom-call | flops 12000000000 | bytes 10000000 | tf_op jit(solution)/shard_map/pallas_call | solution.py:459
  85.6 3.1 %shard_map.51 = (bf16[128,1792]{1,0:T(8,128)(2,1)}, f32[3584,128]{1,0:T(8,128)}) custom-call(bf16[128,1792]{1,0:T(8,128)(2,1)} %get-tuple-element.6.ig, f32[3584,128]{1,0:T(8,128)} %get-tuple-element.7.wg), custom_call_target="tpu_custom_call" | custom-call | tf_op jit(solution)/shard_map/pallas_call | solution.py:492

commit v3 on v2

--- a/solution.py
+++ b/solution.py
@@ -12,35 +12,46 @@
 COLS = 256
 ROWS = 128
 PAD = 16
+STEP = 32
 SPAN = 240.0
-ARRIVE = (-3, 0, 2, 3)
-STRAIGHT = (0, 1)
-LAG = 3
-FIRST = 6
+ARRIVE = (-3, 0, 1, 2)
+LEAVE = (-3, 2, -1, 3)
+NEAR = (-3, 4, -1, 5)
+FIRST = 4
+LAG = 6
+LAST = 8
 
 
 def encode(dst, value):
     n = value.shape[0]
     top = jnp.max(jnp.abs(value), axis=0, keepdims=True)
     scale = (1.0 / jnp.maximum(top, 1e-30)).astype(BF16).astype(F32)
-    for b in range(0, n, 64):
-        u = value[b : b + 64] * scale
+    for b in blocks(n):
+        u = value[b : b + STEP] * scale
         y = jnp.exp2(jnp.abs(u) * SPAN - SPAN / 2)
-        dst[b : b + 64, :] = jnp.where(u < 0.0, -y, y).astype(BF16)
+        dst[b : b + STEP, :] = jnp.where(u < 0.0, -y, y).astype(BF16)
     dst[n:, :] = jnp.broadcast_to(scale, (PAD, value.shape[1])).astype(BF16)
 
 
-def decode(src):
+def decode(src, b):
     n = src.shape[0] - PAD
     scale = src[n:, :].astype(F32)[0:1]
-    y = src[0:n, :].astype(F32)
+    y = src[b : b + STEP, :].astype(F32)
     u = (jnp.log2(jnp.abs(y)) + SPAN / 2) * (1.0 / (SPAN * scale))
     return jnp.where(y < 0.0, -u, u)
 
 
+def blocks(n):
+    return range(0, n, STEP)
+
+
+def straight(tr, j):
+    return True
+
+
 def kernel(
     g_in, h_in, w_in, ig_out, wg_out,
-    G, GS, H, HT, W, WS, igp, igs, igr, igo, wgs, wgr, wgo,
+    G, GS, H, HT, W, WS, igp, igs, igr, igo, sums, wgs, wgr, wgo,
     gA, gBC, gZ4, gZ, gS, hA, hBC, hS, hZ, wS, iR, q, lW, lG, lH, lO, lP,
     sG, sGS, sH, sHS, sW, sI, sWG,
 ):
@@ -92,7 +103,7 @@
 
     def to_ring_y(src, tr, s, j):
         dst = gblk(tr, zsel(s), y, j)
-        if j in STRAIGHT:
+        if straight(tr, j):
             for dev in (to_yp, to_ys, to_y2):
                 send(src, dst, sG, gBC.at[tr, s, j], dev)
         else:
@@ -100,11 +111,11 @@
             send(src, dst, sG, gBC.at[tr, s, j], to_ys)
 
     def own_y(j):
-        to_ring_y(g_in.at[:, in_cols(j)], 0, 0, j)
+        to_ring_y(gblk(0, zh, y, j), 0, 0, j)
 
     def to_ring_x(src, tr, m):
         dst = hblk(m, tr, x)
-        if isinstance(m, int) and m == 0:
+        if tr == 1:
             for dev in (to_xp, to_xs, to_x2):
                 send(src, dst, sH, hBC.at[tr, m], dev)
         else:
@@ -112,16 +123,16 @@
             send(src, dst, sH, hBC.at[tr, m], to_xs)
 
     def own_x(m):
-        to_ring_x(h_in.at[:, cols(m)], 0, m)
+        to_ring_x(hblk(m, 0, x), 0, m)
 
     def own_z(m):
-        send(h_in.at[:, cols(m)], hblk(m, 1, x), sH, hZ.at[m], to_zp)
+        send(hblk(m, 0, x), hblk(m, 1, x), sH, hZ.at[m], to_zp)
 
     def own_z4(j):
-        send(g_in.at[:, in_cols(j)], gblk(0, zh, y, j), sG, gZ4.at[j], to_z4)
+        send(gblk(0, zh, y, j), gblk(0, zh, y, j), sG, gZ4.at[j], to_z4)
 
     def own_gz(j):
-        send(g_in.at[:, in_cols(j)], gblk(1, zh, y, j), sG, gZ.at[0, j], to_zp)
+        send(gblk(0, zh, y, j), gblk(1, zh, y, j), sG, gZ.at[0, j], to_zp)
 
     for j in range(4):
         local(g_in.at[:, in_cols(j)], gblk(0, zh, y, j), lG)
@@ -142,21 +153,23 @@
     def _():
         pl.semaphore_wait(barrier, 10)
 
+    wait(G.at[0:ROWS], lG)
+    wait(H.at[:, 0:ROWS], lH)
+
+    @pl.when(end)
+    def _():
+        own_gz(0)
+        own_z(0)
+        send(gblk(0, zh, y, 0), gblk(1, zh, y, 0), sG, gZ.at[1, 0], to_zd)
+        own_z(1)
+        own_z(2)
+
     own_z4(0)
     own_x(0)
     own_y(0)
     own_x(1)
     own_x(2)
 
-    @pl.when(end)
-    def _():
-        own_gz(0)
-        own_z(0)
-        send(g_in.at[:, in_cols(0)], gblk(1, zh, y, 0), sG, gZ.at[1, 0], to_zd)
-
-    wait(G.at[0:ROWS], lG)
-    wait(H.at[:, 0:ROWS], lH)
-
     blk = G.at[0:ROWS, 0:COLS]
     two = G.at[0 : 2 * ROWS, 0:COLS]
     three = G.at[0 : 3 * ROWS, 0:COLS]
@@ -166,7 +179,7 @@
 
     def full_y(tr, j):
         for s in range(2):
-            wait(three if j in STRAIGHT else two, gBC.at[tr, s, j])
+            wait(three if straight(tr, j) else two, gBC.at[tr, s, j])
 
     def pass_y(tr, s, j):
         z = zsel(s)
@@ -181,12 +194,8 @@
         wait(blk, hZ.at[m])
         to_ring_x(hblk(m, 1, x), 1, m)
 
-    def pass_x(m):
-        wait(blk, hA.at[1, m])
-        send(hblk(m, 1, xs), hblk(m, 1, xs), sH, hBC.at[1, m], to_xp)
-
     def share(tr, m):
-        wait(three if isinstance(m, int) and m == 0 else two, hBC.at[tr, m])
+        wait(three if tr == 1 else two, hBC.at[tr, m])
         own = H.at[m, rows(2 * tr + c, 4 * ROWS)]
         send(own, own, sHS, hS.at[tr, m], to_sib)
 
@@ -194,40 +203,45 @@
         full_y(0, j)
         send(G.at[rows(1 - c, 4 * ROWS), cols(j)], GS.at[:, cols(j)], sGS, gS, to_sib)
 
+    near_x(0)
+
+    @pl.when(end)
+    def _():
+        near_x(1)
+        own_z(3)
+
     wait(blk, gZ4.at[0])
     spread_y(0, 1, 0)
-    own_z4(1)
-
-    @pl.when(end)
-    def _():
-        own_z(1)
-        own_gz(1)
 
     @pl.when(mid)
     def _():
+        near_x(1)
         wait(blk, gZ.at[0, 0])
         spread_y(1, 0, 0)
         wait(blk, gZ.at[1, 0])
         spread_y(1, 1, 0)
         spread_x(0)
 
+    own_z4(1)
     own_z4(2)
+    own_z4(3)
     own_y(1)
-    near_x(1)
+
+    @pl.when(end)
+    def _():
+        own_z(4)
+
+    @pl.when(mid)
+    def _():
+        spread_x(1)
+
+    near_x(2)
     own_x(3)
     share(0, 0)
-    near_x(2)
-
-    @pl.when(end)
-    def _():
-        own_z(2)
 
     @pl.when(mid)
     def _():
-        spread_x(1)
         share(1, 0)
-
-    share_g(0)
 
     def step(s, _):
         def at(k):
@@ -241,9 +255,9 @@
         def _():
             near_x(s + 3)
 
-        @pl.when(end & (s < n_m - 3))
-        def _():
-            own_z(s + 3)
+        @pl.when(end & (s < n_m - 5))
+        def _():
+            own_z(s + 5)
 
         @pl.when(mid & (s < n_m - 2))
         def _():
@@ -251,19 +265,19 @@
 
         @pl.when(s < n_m - 1)
         def _():
+            share(0, s + 1)
+
             @pl.when(mid)
             def _():
-                pass_x(s + 1)
-
-            share(0, s + 1)
-
-        @pl.when(mid & (s >= 1) & (s < n_m))
-        def _():
-            share(1, s)
-
-        @pl.when(mid & (s == 0))
-        def _():
-            full_y(1, 0)
+                share(1, s + 1)
+
+        @at(0)
+        def _():
+            share_g(0)
+
+            @pl.when(mid)
+            def _():
+                full_y(1, 0)
 
         @pl.when(s < n_m)
         def _():
@@ -276,7 +290,7 @@
                 encode(wgs.at[0, s], jnp.dot(HT[s], G[:, 0:COLS], preferred_element_type=F32))
                 send(wgs.at[0, s], wgr.at[0, s], sWG, q.at[0, s], to_zq)
 
-        for j, k in ((1, LAG), (3, ARRIVE[3] + 3)):
+        for j, k in ((1, LAG), (3, LAST)):
 
             @pl.when(mid & (s == k))
             def _():
@@ -289,62 +303,31 @@
             send(wgs.at[1, m], wgr.at[1, m], sWG, q.at[1, m], to_zq)
 
         for j in (1, 2, 3):
-            both = j != 2
-            relay = j not in STRAIGHT
 
             @at(ARRIVE[j] + 2)
             def _():
-                if both and relay:
-
-                    @pl.when(mid)
-                    def _():
-                        pass_y(1, 1, j)
-
                 share_g(j)
-
-            @at(ARRIVE[j] + 1)
-            def _():
-                if both:
-
-                    @pl.when(mid)
-                    def _():
-                        wait(blk, gZ.at[1, j])
-                        spread_y(1, 1, j)
-                        if relay:
-                            pass_y(1, 0, j)
-
-                if relay:
-                    pass_y(0, 1, j)
 
             @at(ARRIVE[j])
             def _():
                 wait(blk, gZ4.at[j])
                 spread_y(0, 1, j)
 
-                if both:
-
-                    @pl.when(end)
-                    def _():
-                        send(gblk(0, 1 - zh, y, j), gblk(1, 1 - zh, y, j), sG, gZ.at[1, j], to_zp)
-
-                    @pl.when(mid)
-                    def _():
-                        wait(blk, gZ.at[0, j])
-                        spread_y(1, 0, j)
-
-                if relay:
-                    pass_y(0, 0, j)
-
-                if j == 1:
-                    own_z4(3)
-                    own_y(2)
-
-                    @pl.when(end)
-                    def _():
-                        own_gz(3)
-
-                if j == 2:
-                    own_y(3)
+                if j < 3:
+                    own_y(j + 1)
+
+        for j in (1, 3):
+
+            @pl.when(end & (s == LEAVE[j]))
+            def _():
+                own_gz(j)
+                send(gblk(0, 1 - zh, y, j), gblk(1, 1 - zh, y, j), sG, gZ.at[1, j], to_zp)
+
+            @pl.when(mid & (s == NEAR[j]))
+            def _():
+                for k in range(2):
+                    wait(blk, gZ.at[k, j])
+                    spread_y(1, k, j)
 
         @at(0)
         def _():
@@ -359,8 +342,8 @@
             wait(WS, wS)
             wait(GS, gS)
 
-        for k in range(2):
-            i = 2 * (s - FIRST) + k
+        for k in range(1):
+            i = s - FIRST
 
             @pl.when((i >= 0) & (i < n_m))
             def _():
@@ -373,28 +356,34 @@
                 encode(igs.at[1, i], igp[i, xs])
                 send(igs.at[1, i], igr.at[1, i], sI, iR.at[1, i], to_xs)
 
-        for k in range(2):
-            l = 2 * (s - FIRST - 1) + k
+        for k in range(1):
+            l = s - FIRST - 2
 
             @pl.when((l >= 0) & (l < n_m))
             def _():
                 wait(igr.at[0, l], iR.at[0, l])
-                encode(igs.at[2, l], igp[l, xp] + decode(igr.at[0, l]))
+                for b in blocks(ROWS):
+                    igp[l, xp, b : b + STEP] += decode(igr.at[0, l], b)
+                encode(igs.at[2, l], igp[l, xp])
                 send(igs.at[2, l], igr.at[2, l], sI, iR.at[2, l], to_xp)
 
-        for k in range(2):
-            n = 2 * (s - FIRST - 2) + k
+        for k in range(1):
+            n = s - FIRST - 4
 
             @pl.when((n >= 0) & (n < n_m))
             def _():
                 wait(igr.at[1, n], iR.at[1, n])
                 wait(igr.at[2, n], iR.at[2, n])
-                igo[n] = (igp[n, x] + decode(igr.at[1, n]) + decode(igr.at[2, n])).astype(BF16)
+                for b in blocks(ROWS):
+                    total = igp[n, x, b : b + STEP] + decode(igr.at[1, n], b) + decode(igr.at[2, n], b)
+                    igo[n, b : b + STEP] = total.astype(BF16)
                 local(igo.at[n], ig_out.at[:, cols(n)], lO)
 
-        def store(u, value):
-            for l in range(2):
-                wgo[u, pl.ds(l, COLS, stride=2), :] = value[:, l * ROWS : (l + 1) * ROWS]
+        def store(u, part, src):
+            for b in blocks(COLS):
+                value = part[b : b + STEP] + decode(src, b)
+                for l in range(2):
+                    wgo[u, pl.ds(2 * b + l, STEP, stride=2), :] = value[:, l * ROWS : (l + 1) * ROWS]
             local(wgo.at[u], wg_out.at[rows(u, 2 * COLS)], lP)
 
         @pl.when(mid & (s >= 4) & (s < n_m + 4))
@@ -402,26 +391,28 @@
             u = s - 4
             part = jnp.dot(HT[u, :, 0 : 8 * ROWS], G[0 : 8 * ROWS, 2 * COLS : 3 * COLS], preferred_element_type=F32)
             wait(wgr.at[0, u], q.at[0, u])
-            encode(wgs.at[2, u], part + decode(wgr.at[0, u]))
+            for b in blocks(COLS):
+                sums[b : b + STEP] = part[b : b + STEP] + decode(wgr.at[0, u], b)
+            encode(wgs.at[2, u], sums[...])
             send(wgs.at[2, u], wgr.at[2, u], sWG, q.at[2, u], to_zp)
 
-        @pl.when(mid & (s >= 6) & (s < n_m + 6))
-        def _():
-            u = s - 6
+        @pl.when(mid & (s >= LAST) & (s < n_m + LAST))
+        def _():
+            u = s - LAST
             part = jnp.dot(HT[u], G[:, 3 * COLS :], preferred_element_type=F32)
             wait(wgr.at[1, u], q.at[1, u])
-            store(u, part + decode(wgr.at[1, u]))
+            store(u, part, wgr.at[1, u])
 
         @pl.when(end & (s >= 6) & (s < n_m + 6))
         def _():
             u = s - 6
             part = jnp.dot(H[u, 0 : 8 * ROWS].T, G[0 : 8 * ROWS, 2 * COLS : 3 * COLS], preferred_element_type=F32)
             wait(wgr.at[2, u], q.at[2, u])
-            store(u, part + decode(wgr.at[2, u]))
+            store(u, part, wgr.at[2, u])
 
         return 0
 
-    lax.fori_loop(0, n_m + 6, step, 0)
+    lax.fori_loop(0, n_m + max(LAST, FIRST + 4), step, 0)
 
     @pl.when(mid)
     def _():
@@ -475,6 +466,7 @@
             vm((3, n_m, ROWS + PAD, COLS), BF16),
             vm((3, n_m, ROWS + PAD, COLS), BF16),
             vm((n_m, ROWS, COLS), BF16),
+            vm((COLS, COLS), F32),
             vm(coded, BF16),
             vm(coded, BF16),
             vm((n_m, 2 * COLS, ROWS), F32),

time: 88.8 us -> 83.4 us (0.939)
  the two profiles are of different devices: /device:TPU:2 before, /device:TPU:32 now
where the time goes in v3:
time: 83.4 us; the launch traced here: 82.6 us
  Pallas kernels  82 us (98%)
    pallas_call x1, Pallas kernels, shards(): pl.pallas_call(kernel, out_shape=(jax.ShapeDtypeStruct((ROWS, n_m * COLS)...  79 us
    pallas_call x1, Pallas kernels, shards(): pl.pallas_call(place, out_shape=tuple((jax.ShapeDtypeStruct(a.shape, a.dt...  3.05 us

profile of v3, /device:TPU:32, one launch (start us, length us, event | category | flops | bytes accessed | tf_op | source)
XLA Modules:
  0.0 82.6 jit_solution(3766770200162346634)
XLA Ops:
  0.6 79.0 %shard_map.50 = (bf16[128,1792]{1,0:T(8,128)(2,1)}, f32[3584,128]{1,0:T(8,128)}) custom-call(bf16[128,1024]{1,0:T(8,128)(2,1)} %g_in.1, bf16[128,1792]{1,0:T(8,128)(2,1)} %h_in.1, bf16[1792,1024]{1,0:T(8,128)(2,1)} %w_in.1), custom_call_target="tpu_custom_call" | custom-call | flops 12000000000 | bytes 10000000 | tf_op jit(solution)/shard_map/pallas_call | solution.py:450
  79.6 3.1 %shard_map.51 = (bf16[128,1792]{1,0:T(8,128)(2,1)}, f32[3584,128]{1,0:T(8,128)}) custom-call(bf16[128,1792]{1,0:T(8,128)(2,1)} %get-tuple-element.6.ig, f32[3584,128]{1,0:T(8,128)} %get-tuple-element.7.wg), custom_call_target="tpu_custom_call" | custom-call | tf_op jit(solution)/shard_map/pallas_call | solution.py:484

commit v4 on v3

--- a/solution.py
+++ b/solution.py
@@ -169,6 +169,8 @@
     own_y(0)
     own_x(1)
     own_x(2)
+    own_x(3)
+    own_x(4)
 
     blk = G.at[0:ROWS, 0:COLS]
     two = G.at[0 : 2 * ROWS, 0:COLS]
@@ -236,7 +238,7 @@
         spread_x(1)
 
     near_x(2)
-    own_x(3)
+    own_x(5)
     share(0, 0)
 
     @pl.when(mid)
@@ -247,9 +249,9 @@
         def at(k):
             return pl.when(s == k)
 
-        @pl.when(s < n_m - 4)
-        def _():
-            own_x(s + 4)
+        @pl.when(s < n_m - 6)
+        def _():
+            own_x(s + 6)
 
         @pl.when(s < n_m - 3)
         def _():
@@ -434,12 +436,22 @@
     wait(wgo, lP)
 
 
-def place(ig, wg, ig_out, wg_out, sems):
-    copies = [pltpu.make_async_copy(ig, ig_out, sems.at[0]), pltpu.make_async_copy(wg, wg_out, sems.at[1])]
-    for copy in copies:
-        copy.start()
-    for copy in copies:
-        copy.wait()
+def place(ig, wg, ig_out, wg_out, ig_held, wg_held, sems):
+    n = sems.shape[0] - 1
+    size = wg.shape[0] // n
+    moves = [(ig, ig_held, ig_out)]
+    for i in range(n):
+        part = pl.ds(i * size, size)
+        moves.append((wg.at[part], wg_held.at[part], wg_out.at[part]))
+    loads = [pltpu.make_async_copy(a, b, sems.at[i]) for i, (a, b, _) in enumerate(moves)]
+    stores = [pltpu.make_async_copy(b, c, sems.at[i]) for i, (_, b, c) in enumerate(moves)]
+    for load in loads:
+        load.start()
+    for load, store in zip(loads, stores):
+        load.wait()
+        store.start()
+    for store in stores:
+        store.wait()
 
 
 def shards(grad_out, hidden, down_weight):
@@ -484,9 +496,9 @@
     ig, wg = pl.pallas_call(
         place,
         out_shape=tuple(jax.ShapeDtypeStruct(a.shape, a.dtype) for a in (ig, wg)),
-        in_specs=[pl.BlockSpec(memory_space=pltpu.VMEM)] * 2,
+        in_specs=[pl.BlockSpec(memory_space=pl.ANY)] * 2,
         out_specs=(pl.BlockSpec(memory_space=pl.ANY),) * 2,
-        scratch_shapes=[dma((2,))],
+        scratch_shapes=[vm(ig.shape, BF16), vm(wg.shape, F32), dma((8,))],
     )(ig, wg)
     return ig, wg.reshape(1, n_m * COLS, 1, COLS)
 

time: 83.4 us -> 81.2 us (0.974)
  Pallas kernels: 82 us -> 80.5 us
    pallas_call x1, Pallas kernels: 79 us -> 78 us  [shards(): pl.pallas_call(kernel, out_shape=(jax.ShapeDtypeStruct((ROWS, n_m * COLS)...]
where the time goes in v4:
time: 81.2 us; the launch traced here: 81.1 us
  Pallas kernels  80.5 us (99%)
    pallas_call x1, Pallas kernels, shards(): pl.pallas_call(kernel, out_shape=(jax.ShapeDtypeStruct((ROWS, n_m * COLS)...  78 us
    pallas_call x1, Pallas kernels, shards(): pl.pallas_call(place, out_shape=tuple((jax.ShapeDtypeStruct(a.shape, a.dt...  2.46 us

profile of v4, /device:TPU:32, one launch (start us, length us, event | category | flops | bytes accessed | tf_op | source)
XLA Modules:
  0.0 81.1 jit_solution(7011951874254602377)
XLA Ops:
  0.6 78.0 %shard_map.50 = (bf16[128,1792]{1,0:T(8,128)(2,1)}, f32[3584,128]{1,0:T(8,128)}) custom-call(bf16[128,1024]{1,0:T(8,128)(2,1)} %g_in.1, bf16[128,1792]{1,0:T(8,128)(2,1)} %h_in.1, bf16[1792,1024]{1,0:T(8,128)(2,1)} %w_in.1), custom_call_target="tpu_custom_call" | custom-call | flops 12000000000 | bytes 10000000 | tf_op jit(solution)/shard_map/pallas_call | solution.py:462
  78.6 2.5 %shard_map.51 = (bf16[128,1792]{1,0:T(8,128)(2,1)}, f32[3584,128]{1,0:T(8,128)}) custom-call(bf16[128,1792]{1,0:T(8,128)(2,1)} %get-tuple-element.6.ig, f32[3584,128]{1,0:T(8,128)} %get-tuple-element.7.wg), custom_call_target="tpu_custom_call" | custom-call | tf_op jit(solution)/shard_map/pallas_call | solution.py:496

commit v5 on v4

--- a/solution.py
+++ b/solution.py
@@ -261,18 +261,6 @@
         def _():
             own_z(s + 5)
 
-        @pl.when(mid & (s < n_m - 2))
-        def _():
-            spread_x(s + 2)
-
-        @pl.when(s < n_m - 1)
-        def _():
-            share(0, s + 1)
-
-            @pl.when(mid)
-            def _():
-                share(1, s + 1)
-
         @at(0)
         def _():
             share_g(0)
@@ -291,6 +279,18 @@
                 HT[s] = H[s].T
                 encode(wgs.at[0, s], jnp.dot(HT[s], G[:, 0:COLS], preferred_element_type=F32))
                 send(wgs.at[0, s], wgr.at[0, s], sWG, q.at[0, s], to_zq)
+
+        @pl.when(mid & (s < n_m - 2))
+        def _():
+            spread_x(s + 2)
+
+        @pl.when(s < n_m - 1)
+        def _():
+            share(0, s + 1)
+
+            @pl.when(mid)
+            def _():
+                share(1, s + 1)
 
         for j, k in ((1, LAG), (3, LAST)):
 

time: 81.2 us -> 80.3 us (0.989)
  Pallas kernels: 80.5 us -> 79.6 us
    pallas_call x1, Pallas kernels: 78 us -> 77.1 us  [shards(): pl.pallas_call(kernel, out_shape=(jax.ShapeDtypeStruct((ROWS, n_m * COLS)...]
where the time goes in v5:
time: 80.3 us; the launch traced here: 80.2 us
  Pallas kernels  79.6 us (99%)
    pallas_call x1, Pallas kernels, shards(): pl.pallas_call(kernel, out_shape=(jax.ShapeDtypeStruct((ROWS, n_m * COLS)...  77.1 us
    pallas_call x1, Pallas kernels, shards(): pl.pallas_call(place, out_shape=tuple((jax.ShapeDtypeStruct(a.shape, a.dt...  2.46 us

profile of v5, /device:TPU:32, one launch (start us, length us, event | category | flops | bytes accessed | tf_op | source)
XLA Modules:
  0.0 80.2 jit_solution(849731581365208976)
XLA Ops:
  0.6 77.1 %shard_map.50 = (bf16[128,1792]{1,0:T(8,128)(2,1)}, f32[3584,128]{1,0:T(8,128)}) custom-call(bf16[128,1024]{1,0:T(8,128)(2,1)} %g_in.1, bf16[128,1792]{1,0:T(8,128)(2,1)} %h_in.1, bf16[1792,1024]{1,0:T(8,128)(2,1)} %w_in.1), custom_call_target="tpu_custom_call" | custom-call | flops 12000000000 | bytes 10000000 | tf_op jit(solution)/shard_map/pallas_call | solution.py:462
  77.8 2.5 %shard_map.51 = (bf16[128,1792]{1,0:T(8,128)(2,1)}, f32[3584,128]{1,0:T(8,128)}) custom-call(bf16[128,1792]{1,0:T(8,128)(2,1)} %get-tuple-element.6.ig, f32[3584,128]{1,0:T(8,128)} %get-tuple-element.7.wg), custom_call_target="tpu_custom_call" | custom-call | tf_op jit(solution)/shard_map/pallas_call | solution.py:496

commit v6 on v5

--- a/solution.py
+++ b/solution.py
@@ -386,7 +386,7 @@
                 value = part[b : b + STEP] + decode(src, b)
                 for l in range(2):
                     wgo[u, pl.ds(2 * b + l, STEP, stride=2), :] = value[:, l * ROWS : (l + 1) * ROWS]
-            local(wgo.at[u], wg_out.at[rows(u, 2 * COLS)], lP)
+            local(wgo.at[u, 0 : 2 * COLS], wg_out.at[rows(u, 2 * COLS)], lP)
 
         @pl.when(mid & (s >= 4) & (s < n_m + 4))
         def _():
@@ -433,7 +433,7 @@
     wait(W, sW)
     wait(igs, sI)
     wait(igo, lO)
-    wait(wgo, lP)
+    wait(wgo.at[:, 0 : 2 * COLS], lP)
 
 
 def place(ig, wg, ig_out, wg_out, ig_held, wg_held, sems):
@@ -481,7 +481,7 @@
             vm((COLS, COLS), F32),
             vm(coded, BF16),
             vm(coded, BF16),
-            vm((n_m, 2 * COLS, ROWS), F32),
+            vm((n_m, 2 * COLS + 8, ROWS), F32),
             dma((2, 2, 4)), dma((2, 2, 4)), dma((4,)), dma((2, 4)), dma,
             dma((2, n_m)), dma((2, n_m)), dma((2, n_m)), dma((n_m,)), dma,
             dma((3, n_m)), dma((3, n_m)),

time: 80.3 us -> 80.3 us (level)
  no operation moved by 1% of the time
where the time goes in v6:
time: 80.3 us; the launch traced here: 80.2 us
  Pallas kernels  79.6 us (99%)
    pallas_call x1, Pallas kernels, shards(): pl.pallas_call(kernel, out_shape=(jax.ShapeDtypeStruct((ROWS, n_m * COLS)...  77.1 us
    pallas_call x1, Pallas kernels, shards(): pl.pallas_call(place, out_shape=tuple((jax.ShapeDtypeStruct(a.shape, a.dt...  2.46 us

profile of v6, /device:TPU:32, one launch (start us, length us, event | category | flops | bytes accessed | tf_op | source)
XLA Modules:
  0.0 80.2 jit_solution(8069512984780301317)
XLA Ops:
  0.6 77.1 %shard_map.50 = (bf16[128,1792]{1,0:T(8,128)(2,1)}, f32[3584,128]{1,0:T(8,128)}) custom-call(bf16[128,1024]{1,0:T(8,128)(2,1)} %g_in.1, bf16[128,1792]{1,0:T(8,128)(2,1)} %h_in.1, bf16[1792,1024]{1,0:T(8,128)(2,1)} %w_in.1), custom_call_target="tpu_custom_call" | custom-call | flops 12000000000 | bytes 10000000 | tf_op jit(solution)/shard_map/pallas_call | solution.py:462
  77.8 2.5 %shard_map.51 = (bf16[128,1792]{1,0:T(8,128)(2,1)}, f32[3584,128]{1,0:T(8,128)}) custom-call(bf16[128,1792]{1,0:T(8,128)(2,1)} %get-tuple-element.6.ig, f32[3584,128]{1,0:T(8,128)} %get-tuple-element.7.wg), custom_call_target="tpu_custom_call" | custom-call | tf_op jit(solution)/shard_map/pallas_call | solution.py:496
